TPU v7x, 256 devices: a whole 4x4x8 slice. The times are simulated.
256 devices in a mesh: slab: 64 (over y_lo, x, z), ang: 4 (over y_hi, core).
Axes of the slice: x: 4, y: 4 (y_hi: 2, y_lo: 2; y = y_hi * 2 + y_lo), z: 8, core: 2. Of those that a mesh axis runs over, the one named last changes fastest.
Arguments:
- volume: float32 [256, 128, 4096], P('slab', 'ang'), may hold values from -6 to 6
- measured: float32 [16, 4096, 4096], P('ang', 'slab'), may hold values from -6 to 6
- incidence: int32 [16, 64, 5], P('ang', 'slab'), may hold values 0 or 1
- row_weights: float32 [16, 5, 4, 64], P('ang'), may hold values from -1.25 to 1.25
- path_table: float32 [2048, 128], P(None, 'ang'), may hold values from -0.5 to 0.5
- subset: int32 [16], replicated, may hold values from 0 to 2047
- gain_map: int32 [64, 64], P('slab'), may hold values from 0 to 4095
- gain_values: float32 [4096], replicated, may hold values from 0.5 to 1.5
Outputs:
- volume_next: float32 [256, 128, 4096], P('slab', 'ang')
- gain_next: float32 [4096], replicated
All inputs are finite; a program needn't handle non-finite values. No bound on the sum of `incidence` on one device may be relied on, other than what follows from the above.
Results may differ from a plain program's by a relative error of at most 0.0003.
Values sent between devices are 32-bit elements; how exact they have to be, the bound alone decides.
No kernel may reach another device: no remote copies, remote signals or barrier semaphores. Data moves between devices by JAX's collectives and lax.ppermute only.
A program may use at most 64 MiB of HBM per device.

v0:
```python
import jax
import jax.numpy as jnp
from jax import lax
from jax.sharding import PartitionSpec as P

HIGH = lax.Precision.HIGHEST


def from_behind(value, axis, by):
    length = lax.axis_size(axis)
    pairs = [(i, i + by) for i in range(length) if 0 <= i + by < length]
    return lax.ppermute(value, axis, pairs)


def padded_2(block, sides, width):
    for axis, dim in sides:
        count = lax.axis_size(axis)
        forward = [(i, i + 1) for i in range(count - 1)]
        backward = [(target, source) for source, target in forward]
        low = lax.ppermute(
            lax.slice_in_dim(block, block.shape[dim] - width, None, axis=dim), axis, forward
        )
        high = lax.ppermute(lax.slice_in_dim(block, 0, width, axis=dim), axis, backward)
        block = jnp.concatenate([low, block, high], axis=dim)
    return block


def tv_from_padded(padded):
    lower = padded[:-1]
    diff_z = padded[1:] - lower
    diff_u = jnp.concatenate([lower[..., 1:], jnp.zeros_like(lower[..., :1])], axis=-1) - lower
    magnitude = jnp.sqrt(diff_z * diff_z + diff_u * diff_u + 0.25)
    flux_z = diff_z / magnitude
    flux_u = diff_u / magnitude
    moved_u = jnp.concatenate([jnp.zeros_like(flux_u[..., :1]), flux_u[..., :-1]], axis=-1)
    return flux_z[:-1] - flux_z[1:] + moved_u[1:] - flux_u[1:]


def local(volume, measured, incidence, row_weights, path_table, subset, gain_map, gain_values):
    reach = (row_weights.shape[1] - 1) // 2
    angles_dev = measured.shape[0]
    block = measured.shape[1]
    columns = measured.shape[2]
    blocks_row = columns // block
    planes = volume.shape[0]
    table_rows = path_table.shape[0]
    params = gain_values.shape[0]
    picker = (subset[:, None] == jnp.arange(table_rows, dtype=jnp.int32)[None, :]).astype(
        jnp.float32
    )
    weights_all = jnp.dot(picker, path_table, precision=HIGH)
    rows_w = weights_all
    line_mine = lax.psum_scatter(
        jnp.einsum("ax,zxu->azu", rows_w, volume, precision=HIGH),
        "ang",
        scatter_dimension=0,
        tiled=True,
    )
    forward_projection = jnp.zeros((angles_dev, block, columns), jnp.float32)
    for offset in range(2 * reach + 1):
        if offset == reach:
            source = line_mine
        else:
            source = from_behind(line_mine, "slab", reach - offset)
        mask = incidence[:, 0, offset].astype(jnp.float32)[:, None, None]
        forward_projection = forward_projection + mask * jnp.einsum(
            "azr,azu->aru", row_weights[:, offset], source, precision=HIGH
        )
    onehot_gain = (gain_map[0][:, None] == jnp.arange(params, dtype=jnp.int32)[None, :]).astype(
        jnp.float32
    )
    block_gain = jnp.dot(onehot_gain, gain_values, precision=HIGH)
    detector_pixel_gain = jnp.repeat(block_gain, block)[None, None, :]
    projection_residual = detector_pixel_gain * forward_projection - measured
    weighted = detector_pixel_gain * projection_residual
    cross = (
        (projection_residual * forward_projection)
        .reshape(angles_dev, block, blocks_row, block)
        .sum(axis=(0, 1, 3))
    )
    energy = (
        (forward_projection * forward_projection)
        .reshape(angles_dev, block, blocks_row, block)
        .sum(axis=(0, 1, 3))
    )
    cross_sum, energy_sum = lax.psum(
        (jnp.dot(cross, onehot_gain, precision=HIGH), jnp.dot(energy, onehot_gain, precision=HIGH)),
        ("slab", "ang"),
    )
    gain_next = gain_values - cross_sum / (energy_sum + 1.0)
    images = jnp.zeros((angles_dev, planes, columns), jnp.float32)
    for offset in range(2 * reach + 1):
        mask = incidence[:, 0, offset].astype(jnp.float32)[:, None, None]
        contrib = (
            jnp.einsum("azr,aru->azu", row_weights[:, offset], weighted, precision=HIGH) * mask
        )
        if offset != reach:
            contrib = from_behind(contrib, "slab", offset - reach)
        images = images + contrib
    rows_w = weights_all
    gradient = jnp.einsum(
        "ax,azu->zxu", rows_w, lax.all_gather(images, "ang", axis=0, tiled=True), precision=HIGH
    )
    padded = padded_2(volume, (("slab", 0),), 1)
    smooth = tv_from_padded(padded)
    volume_next = volume - 0.2 * gradient - 0.2 * smooth
    return (volume_next, gain_next)


def solution(mesh):
    in_specs = (
        P("slab", "ang", None),
        P("ang", "slab", None),
        P("ang", "slab", None),
        P("ang", None, None, None),
        P(None, "ang"),
        P(),
        P("slab", None),
        P(),
    )
    out_specs = (P("slab", "ang", None), P())
    return jax.shard_map(local, mesh=mesh, in_specs=in_specs, out_specs=out_specs, check_vma=False)
```

profile of v0, /device:TPU:1, one launch (start us, length us, event | category | flops | bytes accessed | tf_op | source)
XLA Modules:
  0.0 257.5 jit_solution(8206125433532981096)
XLA Ops:
  7.2 0.9 copy-done
  8.1 0.9 convolution_bitcast_fusion
  9.1 3.7 %fusion.50 = f32[16,4,4096]{2,0,1:T(8,128)} fusion(f32[16,32,1]{1,0,2:T(8,128)S(1)} %convolution_bitcast_fusion, f32[4,32,4096]{2,1,0:T(8,128)} %param.8), kind=kOutput, calls=%fused_computation.83 | convolution fusion | flops 100663296 | bytes 3147776 | tf_op jit(solution)/shard_map/ax,zxu->azu/dot_general | solution.py:54
  12.9 1.1 fusion.49
  14.0 4.4 %collective-permute-start.9 = (f32[1,32,4096]{2,1,0:T(8,128)}, f32[1,32,4096]{2,1,0:T(8,128)S(1)}, u32[]{:S(2)}, u32[]{:S(2)}) collective-permute-start(f32[1,32,4096]{2,1,0:T(8,128)} %get-tuple-element.15), channel_id=1, source_target_pairs={{0,4},{4,8},{8,12},{12,16},{16,20},{20,24},{24,28},{28,32},{32,36}... | collective-permute-start | bytes 1572872 | tf_op jit(solution)/shard_map/ppermute | solution.py:20
  18.4 1.3 collective-permute-start.8
  19.7 0.6 convolution_bitcast_fusion.1
  20.3 0.1 broadcast_in_dim.2
  20.4 0.1 mul.149
  20.5 0.6 dynamic-slice
  21.8 0.2 convert_reduce_fusion.1
  21.9 7.3 %collective-permute-done.9 = f32[1,32,4096]{2,1,0:T(8,128)S(1)} collective-permute-done((f32[1,32,4096]{2,1,0:T(8,128)}, f32[1,32,4096]{2,1,0:T(8,128)S(1)}, u32[]{:S(2)}, u32[]{:S(2)}) %collective-permute-start.9) | collective-permute-done | bytes 524320 | tf_op jit(solution)/shard_map/ppermute | solution.py:20
  29.2 0.8 constant_dynamic-update-slice_fusion.1
  30.0 44.6 %all-reduce.6.cloned.1.call-done = f32[16,4,4096]{2,0,1:T(8,128)} async-done(((f32[16,4,4096]{2,0,1:T(8,128)}), f32[16,4,4096]{2,0,1:T(8,128)}) %all-reduce.6.cloned.1.call-update) | async-done | bytes 1048592
  74.6 1.1 constant_dynamic-slice_fusion
  75.7 0.2 copy.41
  75.9 3.2 %collective-permute-start.1 = (f32[4,4,4096]{2,1,0:T(4,128)S(1)}, f32[4,4,4096]{2,1,0:T(4,128)S(1)}, u32[]{:S(2)}, u32[]{:S(2)}) collective-permute-start(f32[4,4,4096]{2,1,0:T(4,128)S(1)} %copy.41), channel_id=1, source_target_pairs={{0,4},{4,8},{8,12},{12,16},{16,20},{20,24},{24,28},{28,32},{32,36}... | collective-permute-start | bytes 786440 | tf_op jit(solution)/shard_map/ppermute | solution.py:12
  79.1 4.2 %collective-permute-start = (f32[4,4,4096]{2,1,0:T(4,128)S(1)}, f32[4,4,4096]{2,1,0:T(4,128)S(1)}, u32[]{:S(2)}, u32[]{:S(2)}) collective-permute-start(f32[4,4,4096]{2,1,0:T(4,128)S(1)} %copy.41), channel_id=1, source_target_pairs={{0,8},{4,12},{8,16},{12,20},{16,24},{20,28},{24,32},{28,36},{32,40... | collective-permute-start | bytes 786440 | tf_op jit(solution)/shard_map/ppermute | solution.py:12
  83.3 1.3 collective-permute-start.3
  84.6 1.8 collective-permute-start.2
  86.4 3.5 %convolution_multiply_fusion.2 = f32[4,4096,64]{1,2,0:T(8,128)S(1)} fusion(f32[4]{0:T(128)S(1)} %get-tuple-element.5, f32[4,5,4,64]{3,2,1,0:T(4,128)S(1)} %copy-done.5, f32[4,4,4096]{2,0,1:T(4,128)S(1)} %constant_dynamic-slice_fusion), kind=kOutput, calls=%fused_computation.3 | convolution fusion | flops 51380224 | bytes 4465152 | tf_op jit(solution)/shard_map/azr,azu->aru/dot_general | solution.py:66
  89.9 3.5 %convolution_multiply_fusion.3 = f32[4,4096,64]{1,2,0:T(8,128)S(1)} fusion(f32[4,4,4096]{2,1,0:T(4,128)S(1)} %collective-permute-done.1, f32[4]{0:T(128)S(1)} %get-tuple-element.6, f32[4,5,4,64]{3,2,1,0:T(4,128)S(1)} %copy-done.5), kind=kOutput, calls=%fused_computation.4 | convolution fusion | flops 51380224 | bytes 4465152 | tf_op jit(solution)/shard_map/azr,azu->aru/dot_general | solution.py:66
  93.4 3.9 %fusion.2 = f32[4,4096,64]{1,2,0:T(8,128)S(1)} fusion(f32[4,4096,64]{1,2,0:T(8,128)S(1)} %convolution_multiply_fusion.2, f32[4,4096,64]{1,2,0:T(8,128)S(1)} %convolution_multiply_fusion.3, f32[4,4,4096]{2,1,0:T(4,128)S(1)} %collective-permute-done, f32[4]{0:T(128)S(1)} %get-tuple-element.7, f32[4,5,4,64]{3,2,1,0:T(4,128)S(1)} %copy-done.5), kind=kOutput, calls=%fused_computation.7 | convolution fusion | flops 53477376 | bytes 12853760 | tf_op jit(solution)/shard_map/azr,azu->aru/dot_general | solution.py:66
  97.4 1.4 collective-permute-done.3
  98.8 3.7 %convolution_multiply_fusion = f32[4,4096,64]{1,2,0:T(8,128)S(1)} fusion(f32[4,4,4096]{2,1,0:T(4,128)S(1)} %collective-permute-done.3, f32[4]{0:T(128)S(1)} %get-tuple-element.8, f32[4,5,4,64]{3,2,1,0:T(4,128)S(1)} %copy-done.5), kind=kOutput, calls=%fused_computation | convolution fusion | flops 51380224 | bytes 4465152 | tf_op jit(solution)/shard_map/azr,azu->aru/dot_general | solution.py:66
  102.5 4.7 %multiply_reduce_fusion = (f32[4096]{0:T(1024)S(1)}, f32[4096]{0:T(1024)S(1)}, f32[4,64,4096]{2,1,0:T(8,128)S(1)}) fusion(f32[4,64,4096]{2,1,0:T(8,128)S(1)} %copy-done.4, f32[4096]{0:T(1024)S(1)} %mul.149, f32[4,4096,64]{1,2,0:T(8,128)S(1)} %convolution_multiply_fusion, f32[4,4096,64]{1,2,0:T(8,128)S(1)} %fusion.2, ...), kind=kOutput, calls=%fused_computation.24 | convolution fusion | flops 60809216 | bytes 17097216 | tf_op jit(solution)/shard_map/azr,azu->aru/dot_general | solution.py:66
  107.3 2.3 fusion.12
  109.6 2.3 fusion.11
  111.9 2.5 fusion.9
  114.4 2.3 fusion.8
  116.7 1.3 collective-permute-start.4
  118.0 1.3 collective-permute-start.5
  119.3 5.2 %collective-permute-start.6 = (f32[4,4,4096]{2,1,0:T(4,128)S(1)}, f32[4,4,4096]{2,1,0:T(4,128)S(1)}, u32[]{:S(2)}, u32[]{:S(2)}) collective-permute-start(f32[4,4,4096]{2,1,0:T(4,128)S(1)} %fusion.9), channel_id=1, source_target_pairs={{0,4},{4,8},{8,12},{12,16},{16,20},{20,24},{24,28},{28,32},{32,36}... | collective-permute-start | bytes 786440 | tf_op jit(solution)/shard_map/ppermute | solution.py:12
  124.5 6.9 %collective-permute-start.7 = (f32[4,4,4096]{2,1,0:T(4,128)S(1)}, f32[4,4,4096]{2,1,0:T(4,128)S(1)}, u32[]{:S(2)}, u32[]{:S(2)}) collective-permute-start(f32[4,4,4096]{2,1,0:T(4,128)S(1)} %fusion.8), channel_id=1, source_target_pairs={{0,8},{4,12},{8,16},{12,20},{16,24},{20,28},{24,32},{28,36},{32,40... | collective-permute-start | bytes 786440 | tf_op jit(solution)/shard_map/ppermute | solution.py:12
  131.4 0.1 constant_dynamic-update-slice_fusion
  131.6 2.3 slice.86
  133.9 1.9 collective-permute-done.7
  135.8 3.0 %add_add_fusion = f32[4,4,4096]{2,1,0:T(4,128)} fusion(f32[4,4,4096]{2,1,0:T(4,128)S(1)} %collective-permute-done.7, f32[4,4,4096]{2,1,0:T(4,128)S(1)} %collective-permute-done.6, f32[4,4,4096]{2,1,0:T(4,128)S(1)} %collective-permute-done.4, f32[4,4,4096]{2,1,0:T(4,128)S(1)} %collective-permute-done.5, f32[4]{0:T(128)S(1)} %get-tuple-element.5, ...), kind=kOutput, calls=%fused_computation.47 | convolution fusion | flops 50659328 | bytes 5513728 | tf_op jit(solution)/shard_map/azr,aru->azu/dot_general | solution.py:95
  138.9 6.3 %fusion.15 = (f32[5,32,4096]{2,1,0:T(8,128)}, f32[5,32,4096]{2,1,0:T(8,128)}) fusion(f32[5,32,4096]{2,1,0:T(8,128)} %copy-done.3, f32[5,32,4095]{2,1,0:T(8,128)} %slice.86, f32[1,32,4096]{2,1,0:T(8,128)S(1)} %collective-permute-done.8, f32[4,32,4096]{2,1,0:T(8,128)S(1)} %copy-done.1), kind=kLoop, calls=%fused_computation.33 | loop fusion | flops 5898240 | bytes 13106560 | tf_op jit(solution)/shard_map/div | solution.py:33
  145.2 0.1 reduce_sum.24
  145.2 0.1 reduce_sum.36
  145.3 0.1 reduce_sum.25
  145.4 0.1 reduce_sum.37
  145.5 0.5 fusion.21
  146.0 0.5 fusion.20
  146.5 94.9 %all-reduce.3 = (f32[4096]{0:T(1024)S(1)}, f32[4096]{0:T(1024)S(1)}) all-reduce(f32[4096]{0:T(1024)S(1)} %bitcast.88, f32[4096]{0:T(1024)S(1)} %bitcast.89), channel_id=1, replica_groups=mesh['slab'=64,'ang'=4] {'slab','ang'}, use_global_device_ids=true, to_apply=%region_3.0 | all-reduce | flops 8192 | bytes 65536 | tf_op jit(solution)/shard_map/psum | solution.py:86
  241.5 0.6 divide_subtract_fusion
  242.1 8.3 %fusion.7 = f32[4,32,4096]{2,1,0:T(8,128)} fusion(f32[4,32,4096]{2,1,0:T(8,128)S(1)} %copy-done.1, f32[16,32,1]{1,0,2:T(8,128)S(1)} %convolution_bitcast_fusion, f32[5,32,4095]{2,1,0:T(8,128)} %bitcast.87, f32[5,32,4096]{2,1,0:T(8,128)} %get-tuple-element.13, f32[5,32,4096]{2,1,0:T(8,128)} %get-tuple-element.12, f32[16,4,4096]{2,1,0:T(4,128)} %all-gather.2.cloned.1.call-done), kind=kOutput, calls=%fused_computation.13 | convolution fusion | flops 104333312 | bytes 14157184 | tf_op jit(solution)/shard_map/ax,azu->zxu/dot_general | solution.py:101
  (31 shorter events, 0.2 us)
Async XLA Ops:
  7.2 1.0 copy-start
  7.2 5.7 %copy-start.1 = (f32[4,32,4096]{2,1,0:T(8,128)S(1)}, f32[4,32,4096]{2,1,0:T(8,128)}, u32[]{:S(2)}) copy-start(f32[4,32,4096]{2,1,0:T(8,128)} %param.8) | copy-start | bytes 6291460
  7.2 67.4 %all-reduce.6.cloned.1.call-start = ((), (), s32[]{:S(2)}) async-start(), calls=%async_computation.1 | async-start | bytes 2097152
  9.0 10.7 %copy-start.7 = (f32[4096]{0:T(1024)S(1)}, f32[4096]{0:T(1024)}, u32[]{:S(2)}) copy-start(f32[4096]{0:T(1024)} %param.15) | copy-start | bytes 49156
  9.0 10.7 %copy-start.8 = (s32[1,64]{1,0:T(1,128)S(1)}, s32[1,64]{1,0:T(1,128)}, u32[]{:S(2)}) copy-start(s32[1,64]{1,0:T(1,128)} %param.14) | copy-start | bytes 772
  9.1 11.4 %copy-start.9 = (u32[256]{0:T(256)S(1)}, u32[256]{0:T(256)}, u32[]{:S(2)}) copy-start(u32[256]{0:T(256)} %constant.18) | copy-start | bytes 3076
  9.1 12.7 %copy-start.6 = (s32[4,1,5]{2,1,0:T(1,128)S(1)}, s32[4,1,5]{2,1,0:T(1,128)}, u32[]{:S(2)}) copy-start(s32[4,1,5]{2,1,0:T(1,128)} %param.10) | copy-start | bytes 244
  12.8 73.6 %copy-start.5 = (f32[4,5,4,64]{3,2,1,0:T(4,128)S(1)}, f32[4,5,4,64]{3,2,1,0:T(4,128)}, u32[]{:S(2)}) copy-start(f32[4,5,4,64]{3,2,1,0:T(4,128)} %param.11) | copy-start | bytes 61444
  12.8 229.3 %all-gather.2.cloned.1.call-start = ((), (), s32[]{:S(2)}) async-start(), calls=%async_computation | async-start | bytes 1310720 | tf_op jit(solution)/shard_map/all_gather | solution.py:102
  14.0 15.3 %collective-permute-start.9 = (f32[1,32,4096]{2,1,0:T(8,128)}, f32[1,32,4096]{2,1,0:T(8,128)S(1)}, u32[]{:S(2)}, u32[]{:S(2)}) collective-permute-start(f32[1,32,4096]{2,1,0:T(8,128)} %get-tuple-element.15), channel_id=1, source_target_pairs={{0,4},{4,8},{8,12},{12,16},{16,20},{20,24},{24,28},{28,32},{32,36}... | collective-permute-start | bytes 1572872 | tf_op jit(solution)/shard_map/ppermute | solution.py:20
  18.4 120.5 %collective-permute-start.8 = (f32[1,32,4096]{2,1,0:T(8,128)}, f32[1,32,4096]{2,1,0:T(8,128)S(1)}, u32[]{:S(2)}, u32[]{:S(2)}) collective-permute-start(f32[1,32,4096]{2,1,0:T(8,128)} %get-tuple-element.14), channel_id=1, source_target_pairs={{4,0},{8,4},{12,8},{16,12},{20,16},{24,20},{28,24},{32,28},{36,32}... | collective-permute-start | bytes 1572872 | tf_op jit(solution)/shard_map/ppermute | solution.py:23
  75.9 14.0 %collective-permute-start.1 = (f32[4,4,4096]{2,1,0:T(4,128)S(1)}, f32[4,4,4096]{2,1,0:T(4,128)S(1)}, u32[]{:S(2)}, u32[]{:S(2)}) collective-permute-start(f32[4,4,4096]{2,1,0:T(4,128)S(1)} %copy.41), channel_id=1, source_target_pairs={{0,4},{4,8},{8,12},{12,16},{16,20},{20,24},{24,28},{28,32},{32,36}... | collective-permute-start | bytes 786440 | tf_op jit(solution)/shard_map/ppermute | solution.py:12
  79.1 14.3 %collective-permute-start = (f32[4,4,4096]{2,1,0:T(4,128)S(1)}, f32[4,4,4096]{2,1,0:T(4,128)S(1)}, u32[]{:S(2)}, u32[]{:S(2)}) collective-permute-start(f32[4,4,4096]{2,1,0:T(4,128)S(1)} %copy.41), channel_id=1, source_target_pairs={{0,8},{4,12},{8,16},{12,20},{16,24},{20,28},{24,32},{28,36},{32,40... | collective-permute-start | bytes 786440 | tf_op jit(solution)/shard_map/ppermute | solution.py:12
  83.3 15.6 %collective-permute-start.3 = (f32[4,4,4096]{2,1,0:T(4,128)S(1)}, f32[4,4,4096]{2,1,0:T(4,128)S(1)}, u32[]{:S(2)}, u32[]{:S(2)}) collective-permute-start(f32[4,4,4096]{2,1,0:T(4,128)S(1)} %copy.41), channel_id=1, source_target_pairs={{8,0},{12,4},{16,8},{20,12},{24,16},{28,20},{32,24},{36,28},{40,32... | collective-permute-start | bytes 786440 | tf_op jit(solution)/shard_map/ppermute | solution.py:12
  84.6 17.9 %collective-permute-start.2 = (f32[4,4,4096]{2,1,0:T(4,128)S(1)}, f32[4,4,4096]{2,1,0:T(4,128)S(1)}, u32[]{:S(2)}, u32[]{:S(2)}) collective-permute-start(f32[4,4,4096]{2,1,0:T(4,128)S(1)} %copy.41), channel_id=1, source_target_pairs={{4,0},{8,4},{12,8},{16,12},{20,16},{24,20},{28,24},{32,28},{36,32}... | collective-permute-start | bytes 786440 | tf_op jit(solution)/shard_map/ppermute | solution.py:12
  97.4 5.1 %copy-start.4 = (f32[4,64,4096]{2,1,0:T(8,128)S(1)}, f32[4,64,4096]{2,1,0:T(8,128)}, u32[]{:S(2)}) copy-start(f32[4,64,4096]{2,1,0:T(8,128)} %param.9) | copy-start | bytes 12582916
  114.4 17.0 %copy-start.2 = (f32[5,32,4096]{2,1,0:T(8,128)S(1)}, f32[5,32,4096]{2,1,0:T(8,128)}, u32[]{:S(2)}) copy-start(f32[5,32,4096]{2,1,0:T(8,128)} %constant_dynamic-update-slice_fusion.1) | copy-start | bytes 7864324
  116.7 17.2 %collective-permute-start.4 = (f32[4,4,4096]{2,1,0:T(4,128)S(1)}, f32[4,4,4096]{2,1,0:T(4,128)S(1)}, u32[]{:S(2)}, u32[]{:S(2)}) collective-permute-start(f32[4,4,4096]{2,1,0:T(4,128)S(1)} %fusion.12), channel_id=1, source_target_pairs={{8,0},{12,4},{16,8},{20,12},{24,16},{28,20},{32,24},{36,28},{40,32... | collective-permute-start | bytes 786440 | tf_op jit(solution)/shard_map/ppermute | solution.py:12
  118.0 15.9 %collective-permute-start.5 = (f32[4,4,4096]{2,1,0:T(4,128)S(1)}, f32[4,4,4096]{2,1,0:T(4,128)S(1)}, u32[]{:S(2)}, u32[]{:S(2)}) collective-permute-start(f32[4,4,4096]{2,1,0:T(4,128)S(1)} %fusion.11), channel_id=1, source_target_pairs={{4,0},{8,4},{12,8},{16,12},{20,16},{24,20},{28,24},{32,28},{36,32}... | collective-permute-start | bytes 786440 | tf_op jit(solution)/shard_map/ppermute | solution.py:12
  119.3 14.6 %collective-permute-start.6 = (f32[4,4,4096]{2,1,0:T(4,128)S(1)}, f32[4,4,4096]{2,1,0:T(4,128)S(1)}, u32[]{:S(2)}, u32[]{:S(2)}) collective-permute-start(f32[4,4,4096]{2,1,0:T(4,128)S(1)} %fusion.9), channel_id=1, source_target_pairs={{0,4},{4,8},{8,12},{12,16},{16,20},{20,24},{24,28},{28,32},{32,36}... | collective-permute-start | bytes 786440 | tf_op jit(solution)/shard_map/ppermute | solution.py:12
  124.5 11.3 %collective-permute-start.7 = (f32[4,4,4096]{2,1,0:T(4,128)S(1)}, f32[4,4,4096]{2,1,0:T(4,128)S(1)}, u32[]{:S(2)}, u32[]{:S(2)}) collective-permute-start(f32[4,4,4096]{2,1,0:T(4,128)S(1)} %fusion.8), channel_id=1, source_target_pairs={{0,8},{4,12},{8,16},{12,20},{16,24},{20,28},{24,32},{28,36},{32,40... | collective-permute-start | bytes 786440 | tf_op jit(solution)/shard_map/ppermute | solution.py:12
  131.5 2.3 copy-start.3
Sparse Core Ops, SparseCore 0:
  12.9 61.6 all-reduce.5
  139.0 38.0 all-gather.1
where the time goes:
time: 261 us; the launch traced here: 257 us
  blocking collectives  94.9 us (36%)
  waiting for transfers between devices  55.3 us (21%)
  matrix products  46.4 us (18%)
  starting transfers between devices  30.9 us (12%)
  between operations  15.3 us (6%)
  local copies, waits for them, and re-layouts  7.49 us (3%)
  other arithmetic  7.28 us (3%)
    psum x1, blocking collectives, local(): lax.psum((jnp.dot(cross, onehot_gain, precision=HIGH), jnp.dot(energy, on...  94.9 us
    unnamed x3, waiting for transfers between devices  44.6 us
    ppermute x8, starting transfers between devices, from_behind(): return lax.ppermute(value, axis, pairs)  25.1 us
    dot_general x5, matrix products, local(): jnp.einsum('azr,azu->aru', row_weights[:, offset], source, precision=HIGH)  19.3 us
    dot_general x5, matrix products, local(): jnp.einsum('azr,aru->azu', row_weights[:, offset], weighted, precision=HIGH)  12.5 us
    dot_general x1, matrix products, local(): jnp.einsum('ax,azu->zxu', rows_w, lax.all_gather(images, 'ang', axis=0, t...  8.29 us
    ppermute x1, waiting for transfers between devices, padded_2(): lax.ppermute(lax.slice_in_dim(block, block.shape[dim] - width, None, axis...  7.27 us
    div x1, other arithmetic, tv_from_padded(): flux_z = diff_z / magnitude  6.26 us
  transfers between devices with their start and end apart: 12, of which 4 were waited for; matrix products, arithmetic and copies ran while one was open for 18% of the time, Pallas kernels for 0%

commit v1 on v0

v1 whole, which is shorter than its diff:
```python
import functools

import jax
import jax.numpy as jnp
from jax import lax
from jax.experimental import pallas as pl
from jax.experimental.pallas import tpu as pltpu
from jax.sharding import PartitionSpec as P

F32 = jnp.float32
BF16 = jnp.bfloat16
MIB = 1024 * 1024
LINES_LIMIT = 50


def split(value):
    high = value.astype(BF16)
    low = (value - high.astype(F32)).astype(BF16)
    return high, low


def params(limit=12):
    return pltpu.CompilerParams(vmem_limit_bytes=limit * MIB)


def cost(flops, moved):
    return pl.CostEstimate(flops=flops, bytes_accessed=moved, transcendentals=0)


def full(shape):
    return pl.BlockSpec(shape, lambda i: (0,) * len(shape))


def heading():
    return 1 - 2 * (lax.axis_index("ang") & 1)


def order_of(offsets):
    reach = offsets // 2
    ahead = heading()
    return (reach - ahead, reach + ahead, reach - 2 * ahead, reach + 2 * ahead, reach)


def lines_kernel(steps, subset_in, table_in, volume, *rest):
    outs, weights_out, leading, trailing = rest[:4], rest[4], rest[5], rest[6]
    held, table, subset, sems = rest[7:]
    planes, depth, columns = held.shape
    width = columns // steps
    groups = 4
    angles = weights_out.shape[0] // planes
    each = angles // groups

    def copy(step):
        run = pl.ds(step * width, width)
        return pltpu.make_async_copy(
            volume.at[:, :, run], held.at[:, :, run], sems.at[step]
        )

    subset_copy = pltpu.make_async_copy(subset_in, subset, sems.at[steps])
    table_copy = pltpu.make_async_copy(table_in, table, sems.at[steps + 1])
    subset_copy.start()
    table_copy.start()
    for step in range(steps):
        copy(step).start()

    subset_copy.wait()
    me = lax.axis_index("ang")
    slot = lax.broadcasted_iota(jnp.int32, (angles, 1), 0)
    wanted = jnp.zeros((angles, 1), jnp.int32)
    for group, owner in enumerate((3 - me, me ^ 1, me ^ 2, me)):
        for i in range(each):
            wanted = jnp.where(slot == group * each + i, subset[owner * each + i], wanted)
    entries = table.shape[1]
    onehot = jnp.where(
        lax.broadcasted_iota(jnp.int32, (angles, entries), 1) == wanted, 1.0, 0.0
    ).astype(BF16)
    picked = jnp.zeros((angles, depth), F32)
    table_copy.wait()
    rest_of = table[...]
    for _ in range(3):
        part = rest_of.astype(BF16)
        picked = picked + lax.dot_general(
            onehot, part, (((1,), (1,)), ((), ())), preferred_element_type=F32
        )
        rest_of = rest_of - part.astype(F32)
    wide = jnp.concatenate([picked] * planes, axis=1)
    mask = (
        lax.broadcasted_iota(jnp.int32, (planes, planes * depth), 0)
        == lax.broadcasted_iota(jnp.int32, (planes, planes * depth), 1) // depth
    )
    for angle in range(angles):
        row = jnp.broadcast_to(wide[angle : angle + 1], mask.shape)
        weights_out[angle * planes : (angle + 1) * planes, :] = jnp.where(mask, row, 0.0)
    high_w, low_w = split(weights_out[...])
    both_w = jnp.concatenate([high_w, low_w], axis=0)
    count = angles * planes
    size = count // groups
    first = jnp.where(heading() > 0, planes - 1, 0)
    for step in range(steps):
        copy(step).wait()
        run = slice(step * width, (step + 1) * width)
        leading[:, run] = held[first, :, run]
        trailing[:, run] = held[planes - 1 - first, :, run]
        high, low = split(held[:, :, run].reshape(planes * depth, width))
        main = jnp.dot(both_w, high, preferred_element_type=F32)
        lines = (
            main[:count]
            + main[count:]
            + jnp.dot(high_w, low, preferred_element_type=F32)
        )
        for group in range(groups):
            outs[group][:, run] = lines[group * size : (group + 1) * size]


def make_lines(subset, path_table, volume, steps=4):
    planes, depth, columns = volume.shape
    angles = subset.shape[0]
    rows = angles * planes // 4
    vmem = pl.BlockSpec(memory_space=pltpu.VMEM)
    return pl.pallas_call(
        functools.partial(lines_kernel, steps),
        in_specs=[pl.BlockSpec(memory_space=pl.ANY)] * 3,
        out_specs=[vmem] * 7,
        out_shape=[jax.ShapeDtypeStruct((rows, columns), F32)] * 4
        + [jax.ShapeDtypeStruct((angles * planes, planes * depth), F32)]
        + [jax.ShapeDtypeStruct((depth, columns), F32)] * 2,
        scratch_shapes=[
            pltpu.VMEM((planes, depth, columns), F32),
            pltpu.VMEM(path_table.shape[::-1], F32),
            pltpu.SMEM(subset.shape, jnp.int32),
            pltpu.SemaphoreType.DMA((steps + 2,)),
        ],
        compiler_params=params(LINES_LIMIT),
        cost_estimate=cost(6 * angles * planes * depth * columns, 3 * MIB),
        name="lines",
    )(subset, path_table.T, volume)


def add_kernel(count, *refs):
    total = refs[0][...]
    for ref in refs[1:count]:
        total = total + ref[...]
    out = refs[-1]
    out[...] = total


def add_through_kernel(count, passed, *refs):
    add_kernel(count, *refs[: len(refs) - passed])


def add(*values, after=(), through=()):
    vmem = pl.BlockSpec(memory_space=pltpu.VMEM)
    anywhere = pl.BlockSpec(memory_space=pl.ANY)
    count = len(values) + len(after)
    outs = pl.pallas_call(
        functools.partial(add_through_kernel, len(values), len(through)),
        in_specs=[vmem] * len(values) + [anywhere] * (len(after) + len(through)),
        out_specs=[vmem] + [anywhere] * len(through),
        out_shape=[jax.ShapeDtypeStruct(values[0].shape, F32)]
        + [jax.ShapeDtypeStruct(value.shape, value.dtype) for value in through],
        input_output_aliases={count + i: 1 + i for i in range(len(through))},
        compiler_params=params(8),
        cost_estimate=cost(values[0].size * len(values), values[0].size * 4 * len(values)),
        name="add",
    )(*values, *after, *through)
    return outs if through else outs[0]


def prepare_kernel(slabs, incidence, row_weights, gain_map, gain_values, *rest):
    ahead, back, gains, onehot = rest[-6:-2]
    flat = rest[-1]
    angles, offsets, planes, block = row_weights.shape
    flat[...] = jnp.zeros_like(flat)
    slab = lax.axis_index("slab")
    for spot, offset in enumerate(order_of(offsets)):
        other = slab + offset - offsets // 2
        inside = jnp.where((other >= 0) & (other < slabs), 1, 0)
        for angle in range(angles):
            factor = (incidence[angle, 0, offset] * inside).astype(F32)
            at = (spot * angles + angle) * planes
            flat[at : at + planes, angle * block : (angle + 1) * block] = (
                row_weights[angle, offset] * factor
            )
    high, low = split(flat[...])
    back[...] = jnp.concatenate([high, low], axis=0)
    turned = flat[...].T
    high, low = split(turned)
    ahead[...] = jnp.concatenate([high, low, high], axis=1)
    lane = lax.broadcasted_iota(jnp.int32, (1, 2 * block), 1)
    first = lane < block
    spot = lane & (block - 1)
    blocks = gain_map.shape[1]
    for i in range(blocks // 2):
        low_gain = gain_values[gain_map[0, 2 * i]]
        high_gain = gain_values[gain_map[0, 2 * i + 1]]
        gains[:, 2 * i * block : 2 * (i + 1) * block] = jnp.where(first, low_gain, high_gain)
    for i in range(blocks):
        index = gain_map[0, i]
        target = jnp.where(first, index // block, index & (block - 1))
        onehot[i : i + 1, :] = (spot == target).astype(F32)


def prepare(incidence, row_weights, gain_map, gain_values, slabs, after, through):
    angles, offsets, planes, block = row_weights.shape
    rows = offsets * angles * planes
    columns = gain_map.shape[1] * block
    smem = pl.BlockSpec(memory_space=pltpu.SMEM)
    anywhere = pl.BlockSpec(memory_space=pl.ANY)
    vmem = pl.BlockSpec(memory_space=pltpu.VMEM)
    return pl.pallas_call(
        functools.partial(prepare_kernel, slabs),
        in_specs=[smem, vmem, smem, smem] + [anywhere] * (len(after) + 1),
        out_specs=[vmem] * 4 + [anywhere],
        out_shape=[
            jax.ShapeDtypeStruct((angles * block, 3 * rows), BF16),
            jax.ShapeDtypeStruct((2 * rows, angles * block), BF16),
            jax.ShapeDtypeStruct((1, columns), F32),
            jax.ShapeDtypeStruct((gain_map.shape[1], 2 * block), F32),
            jax.ShapeDtypeStruct(through.shape, F32),
        ],
        input_output_aliases={4 + len(after): 4},
        scratch_shapes=[pltpu.VMEM((rows, angles * block), F32)],
        compiler_params=params(),
        cost_estimate=cost(1000000, 1 * MIB),
        name="prepare",
    )(incidence, row_weights, gain_map, gain_values, *after, through)


def detector_kernel(offsets, ahead, back, gains, measured, *refs):
    lines = refs[:offsets]
    outs = refs[-1 - offsets : -1]
    sums = refs[-1]
    angles, block, width = measured.shape
    high, low = split(jnp.concatenate([line[...] for line in lines], axis=0))
    stacked = jnp.concatenate([high, high, low], axis=0)
    forward = jnp.dot(ahead[...], stacked, preferred_element_type=F32)
    gain = gains[...]
    residual = gain * forward - measured[...].reshape(angles * block, width)
    weighted = gain * residual
    cross = jnp.sum(residual * forward, axis=0, keepdims=True)
    energy = jnp.sum(forward * forward, axis=0, keepdims=True)
    sums[...] = jnp.concatenate([cross, energy], axis=0)
    high, low = split(weighted)
    count = back.shape[0] // 2
    main = jnp.dot(back[...], high, preferred_element_type=F32)
    planes = (
        main[:count] + main[count:] + jnp.dot(back[:count], low, preferred_element_type=F32)
    )
    size = count // offsets
    for offset in range(offsets):
        outs[offset][...] = planes[offset * size : (offset + 1) * size]


def detector(ahead, back, gains, measured, lines, after=(), steps=8):
    offsets = len(lines)
    angles, block, columns = measured.shape
    rows = lines[0].shape[0]
    width = columns // steps
    piece = pl.BlockSpec((rows, width), lambda i: (0, i))
    return pl.pallas_call(
        functools.partial(detector_kernel, offsets),
        grid=(steps,),
        in_specs=[
            full(ahead.shape),
            full(back.shape),
            pl.BlockSpec((1, width), lambda i: (0, i)),
            pl.BlockSpec((angles, block, width), lambda i: (0, 0, i)),
        ]
        + [piece] * offsets
        + [pl.BlockSpec(memory_space=pl.ANY)] * len(after),
        out_specs=[piece] * offsets + [pl.BlockSpec((2, width), lambda i: (0, i))],
        out_shape=[jax.ShapeDtypeStruct((rows, columns), F32)] * offsets
        + [jax.ShapeDtypeStruct((2, columns), F32)],
        compiler_params=params(),
        cost_estimate=cost(12 * angles * block * rows * offsets * columns // angles, 8 * MIB),
        name="detector",
    )(ahead, back, gains, measured, *lines, *after)


def scatter_kernel(sums, onehot, out):
    blocks, wide = onehot.shape
    block = wide // 2
    columns = sums.shape[1]
    mine = (
        lax.broadcasted_iota(jnp.int32, (blocks, columns), 1) // block
        == lax.broadcasted_iota(jnp.int32, (blocks, columns), 0)
    )
    cross = jnp.sum(jnp.where(mine, sums[0:1, :], 0.0), axis=1, keepdims=True)
    energy = jnp.sum(jnp.where(mine, sums[1:2, :], 0.0), axis=1, keepdims=True)
    lows = onehot[:, block:]
    value = jnp.concatenate([cross * lows, energy * lows], axis=1)
    first = value.astype(BF16)
    rest = value - first.astype(F32)
    second = rest.astype(BF16)
    third = (rest - second.astype(F32)).astype(BF16)
    highs = onehot[:, :block].astype(BF16).astype(F32).T.astype(BF16)
    out[...] = jnp.dot(
        jnp.concatenate([highs] * 3, axis=1),
        jnp.concatenate([first, second, third], axis=0),
        preferred_element_type=F32,
    )


def scatter(sums, onehot):
    blocks, wide = onehot.shape
    return pl.pallas_call(
        scatter_kernel,
        out_shape=jax.ShapeDtypeStruct((blocks, wide), F32),
        compiler_params=params(),
        cost_estimate=cost(4 * blocks * sums.shape[1], MIB // 8),
        name="scatter",
    )(sums, onehot)


def smooth_kernel(slabs, volume, leading, trailing, *rest):
    out = rest[-1]
    planes, rows, columns = volume.shape
    swap = heading() < 0
    slab = lax.axis_index("slab")
    below = jnp.where(swap, trailing[...], leading[...])
    above = jnp.where(swap, leading[...], trailing[...])
    below = jnp.where(slab == 0, 0.0, below)
    above = jnp.where(slab == slabs - 1, 0.0, above)
    lane = lax.broadcasted_iota(jnp.int32, (rows, columns), 1)
    last = lane == columns - 1
    begin = lane == 0

    def fluxes(here, after):
        ahead = jnp.where(last, 0.0, pltpu.roll(here, columns - 1, 1))
        diff_z = after - here
        diff_u = ahead - here
        scale = lax.rsqrt(diff_z * diff_z + diff_u * diff_u + 0.25)
        return diff_z * scale, diff_u * scale

    flux_below, _ = fluxes(below, volume[0])
    for plane in range(planes):
        here = volume[plane]
        after = volume[plane + 1] if plane + 1 < planes else above
        flux_z, flux_u = fluxes(here, after)
        moved = jnp.where(begin, 0.0, pltpu.roll(flux_u, 1, 1))
        out[plane] = here - 0.2 * (flux_below - flux_z + moved - flux_u)
        flux_below = flux_z


def smooth(volume, leading, trailing, slabs, after):
    planes, depth, columns = volume.shape
    rows = 8
    block = pl.BlockSpec((planes, rows, columns), lambda i: (0, i, 0))
    edge = pl.BlockSpec((rows, columns), lambda i: (i, 0))
    return pl.pallas_call(
        functools.partial(smooth_kernel, slabs),
        grid=(depth // rows,),
        in_specs=[block, edge, edge] + [pl.BlockSpec(memory_space=pl.ANY)] * len(after),
        out_specs=block,
        out_shape=jax.ShapeDtypeStruct(volume.shape, F32),
        compiler_params=params(),
        cost_estimate=cost(40 * planes * depth * columns, 5 * MIB),
        name="smooth",
    )(volume, leading, trailing, *after)


def update_kernel(count, weights, base, *refs):
    images, out, turned = refs[:count], refs[-2], refs[-1]
    planes, depth, width = base.shape

    @pl.when(pl.program_id(0) == 0)
    def _():
        high, low = split(weights[...].T)
        turned[...] = jnp.concatenate([high, low, high], axis=1)

    high, low = split(jnp.concatenate([image[...] for image in images], axis=0))
    gradient = jnp.dot(
        turned[...], jnp.concatenate([high, high, low], axis=0), preferred_element_type=F32
    )
    out[...] = base[...] - 0.2 * gradient.reshape(planes, depth, width)


def update(weights, base, images, after=(), steps=4):
    planes, depth, columns = base.shape
    width = columns // steps
    rows = images[0].shape[0]
    block = pl.BlockSpec((planes, depth, width), lambda i: (0, 0, i))
    return pl.pallas_call(
        functools.partial(update_kernel, len(images)),
        grid=(steps,),
        in_specs=[full(weights.shape), block]
        + [pl.BlockSpec((rows, width), lambda i: (0, i))] * len(images)
        + [pl.BlockSpec(memory_space=pl.ANY)] * len(after),
        out_specs=block,
        out_shape=jax.ShapeDtypeStruct(base.shape, F32),
        scratch_shapes=[pltpu.VMEM((weights.shape[1], 3 * weights.shape[0]), BF16)],
        compiler_params=params(),
        cost_estimate=cost(6 * weights.size * columns, 5 * MIB),
        name="update",
    )(weights, base, *images, *after)


def local(volume, measured, incidence, row_weights, path_table, subset, gain_map, gain_values):
    slabs = lax.axis_size("slab")
    parts = lax.axis_size("ang")
    both = ("slab", "ang")

    def neighbours(turn):
        pairs = []
        for slab in range(slabs):
            for part in range(parts):
                target = slab + 1 - 2 * ((part + turn) % 2)
                if 0 <= target < slabs:
                    pairs.append((slab * parts + part, target * parts + part))
                else:
                    pairs.append((slab * parts + part, slab * parts + (part ^ 1)))
        return pairs

    def flipped(bit):
        return [(i, i ^ bit) for i in range(slabs * parts)]

    def send(value, pairs):
        return lax.ppermute(value, both, pairs)

    first, second = neighbours(0), neighbours(1)
    mates, partners = flipped(1), flipped(2)

    mate_far, mate_near, far, near, weights, leading, trailing = make_lines(
        subset, path_table, volume
    )
    far = send(add(far, send(mate_far, mates)), partners)
    line = add(near, send(mate_near, mates), far)

    line_0 = send(line, first)
    line_1 = send(line, second)
    line_2 = send(line_0, first)
    line_3 = send(line_1, second)

    ahead, back, gains, onehot, leading = prepare(
        incidence, row_weights, gain_map, gain_values, slabs, (line_0, line_1), leading
    )
    leading = send(leading, first)

    *terms, sums = detector(
        ahead, back, gains, measured, (line_0, line_1, line_2, line_3, line)
    )
    to_first = send(terms[3], first)
    to_second = send(terms[2], second)

    totals = scatter(sums, onehot)
    totals = totals + send(totals, mates)

    to_first_next = add(terms[1], to_first, after=(totals,))
    to_second_next, trailing = add(
        terms[0], to_second, after=(totals, leading), through=(trailing,)
    )
    totals = add(totals, send(totals, partners), after=(to_first_next, to_second_next))
    from_first = send(to_first_next, first)
    from_second = send(to_second_next, second)
    trailing = send(trailing, second)

    totals = totals + send(totals, flipped(8 * parts))

    own = add(terms[4], from_first, from_second, after=(totals,))
    mate_own = send(own, mates)
    other = send(own, partners)
    mate_other = send(other, mates)

    base = smooth(volume, leading, trailing, slabs, after=(own,))
    totals = add(totals, send(totals, flipped(16 * parts)), after=(own, base))
    for bit in (32, 1, 2, 4):
        totals = totals + send(totals, flipped(bit * parts))

    volume_next = update(weights, base, (mate_other, mate_own, other, own))

    side = totals.shape[1] // 2
    gain_next = gain_values - (totals[:, :side] / (totals[:, side:] + 1.0)).reshape(-1)
    return volume_next, gain_next


def solution(mesh):
    in_specs = (
        P("slab", "ang", None),
        P("ang", "slab", None),
        P("ang", "slab", None),
        P("ang", None, None, None),
        P(None, "ang"),
        P(),
        P("slab", None),
        P(),
    )
    out_specs = (P("slab", "ang", None), P())
    return jax.shard_map(local, mesh=mesh, in_specs=in_specs, out_specs=out_specs, check_vma=False)
```

time: 261 us -> 112 us (0.43)
  the two profiles are of different devices: /device:TPU:1 before, /device:TPU:8 now
where the time goes in v1:
time: 112 us; the launch traced here: 111 us
  starting transfers between devices  46.1 us (41%)
  waiting for transfers between devices  46 us (41%)
  Pallas kernels  14.5 us (13%)
  local copies, waits for them, and re-layouts  3.19 us (3%)
    ppermute x24, starting transfers between devices, send(): return lax.ppermute(value, both, pairs)  46.1 us
    ppermute x24, waiting for transfers between devices, send(): return lax.ppermute(value, both, pairs)  46 us
    pallas_call x1, Pallas kernels, detector(): pl.pallas_call(functools.partial(detector_kernel, offsets), grid=(steps,)...  4.74 us
    unnamed x18, local copies, waits for them, and re-layouts  3.11 us
    pallas_call x1, Pallas kernels, update(): pl.pallas_call(functools.partial(update_kernel, len(images)), grid=(steps...  2.68 us
    pallas_call x1, Pallas kernels, smooth(): pl.pallas_call(functools.partial(smooth_kernel, slabs), grid=(depth // ro...  2.63 us
    pallas_call x1, Pallas kernels, make_lines(): pl.pallas_call(functools.partial(lines_kernel, steps), in_specs=[pl.Block...  2.48 us
  transfers between devices with their start and end apart: 24, of which 15 were waited for; matrix products, arithmetic and copies ran while one was open for 1% of the time, Pallas kernels for 8%

profile of v1, /device:TPU:8, one launch (start us, length us, event | category | flops | bytes accessed | tf_op | source)
XLA Modules:
  0.0 111.4 jit_solution(11649961545115952594)
XLA Ops:
  0.6 0.9 copy-done.2
  1.6 0.7 copy-done.7
  2.2 2.5 %lines.1 = (f32[16,4096]{1,0:T(8,128)S(1)}, f32[16,4096]{1,0:T(8,128)S(1)}, f32[16,4096]{1,0:T(8,128)S(1)}, f32[16,4096]{1,0:T(8,128)S(1)}, f32[64,128]{1,0:T(8,...) custom-call(s32[16]{0:T(128)S(1)} %copy-done.7, f32[32,2048]{1,0:T(8,128)S(1)} %bitcast.1, f32[4,32,4096]{2,1,0:T(8,128)} %volume.3), custom_call_target="tpu_custom_call" | custom-call | flops 50331648 | bytes 3145728 | tf_op jit(solution)/shard_map/lines/pallas_call | solution.py:120
  4.7 0.1 collective-permute-start.1
  4.8 0.5 collective-permute-start
  5.3 1.0 collective-permute-done.1.refs_1_
  6.4 2.4 %collective-permute-start.2 = (f32[16,4096]{1,0:T(8,128)S(1)}, f32[16,4096]{1,0:T(8,128)S(1)}, u32[]{:S(2)}, u32[]{:S(2)}) collective-permute-start(f32[16,4096]{1,0:T(8,128)S(1)} %add.43), channel_id=1, source_target_pairs={{0,2},{1,3},{2,0},{3,1},{4,6},{5,7},{6,4},{7,5},{8,10},{9,11},{10,... | collective-permute-start | bytes 786440 | tf_op jit(solution)/shard_map/ppermute | solution.py:418
  8.8 7.6 %collective-permute-done.2.refs_2_ = f32[16,4096]{1,0:T(8,128)S(1)} collective-permute-done((f32[16,4096]{1,0:T(8,128)S(1)}, f32[16,4096]{1,0:T(8,128)S(1)}, u32[]{:S(2)}, u32[]{:S(2)}) %collective-permute-start.2) | collective-permute-done | bytes 262176 | tf_op jit(solution)/shard_map/ppermute | solution.py:418
  16.4 2.0 %collective-permute-start.3 = (f32[16,4096]{1,0:T(8,128)S(1)}, f32[16,4096]{1,0:T(8,128)S(1)}, u32[]{:S(2)}, u32[]{:S(2)}) collective-permute-start(f32[16,4096]{1,0:T(8,128)S(1)} %add.44.refs_4_), channel_id=1, source_target_pairs={{0,4},{1,0},{2,6},{3,2},{4,8},{5,1},{6,10},{7,3},{8,12},{9,5},{10,... | collective-permute-start | bytes 786440 | tf_op jit(solution)/shard_map/ppermute | solution.py:418
  18.4 6.1 %collective-permute-start.4 = (f32[16,4096]{1,0:T(8,128)S(1)}, f32[16,4096]{1,0:T(8,128)S(1)}, u32[]{:S(2)}, u32[]{:S(2)}) collective-permute-start(f32[16,4096]{1,0:T(8,128)S(1)} %add.44.refs_4_), channel_id=1, source_target_pairs={{0,1},{1,5},{2,3},{3,7},{4,0},{5,9},{6,2},{7,11},{8,4},{9,13},{10,... | collective-permute-start | bytes 786440 | tf_op jit(solution)/shard_map/ppermute | solution.py:418
  24.5 4.3 %collective-permute-done.3.rest_0_.refs_0_ = f32[16,4096]{1,0:T(8,128)S(1)} collective-permute-done((f32[16,4096]{1,0:T(8,128)S(1)}, f32[16,4096]{1,0:T(8,128)S(1)}, u32[]{:S(2)}, u32[]{:S(2)}) %collective-permute-start.3) | collective-permute-done | bytes 262176 | tf_op jit(solution)/shard_map/ppermute | solution.py:418
  28.8 0.7 collective-permute-done.4.rest_1_.refs_1_
  29.4 6.7 %collective-permute-start.7 = (f32[16,4096]{1,0:T(8,128)S(1)}, f32[16,4096]{1,0:T(8,128)S(1)}, u32[]{:S(2)}, u32[]{:S(2)}) collective-permute-start(f32[16,4096]{1,0:T(8,128)S(1)} %collective-permute-done.4.rest_1_.refs_1_), channel_id=1, source_target_pairs={{0,1},{1,5},{2,3},{3,7},{4,0},{5,9},{6,2},{7,11},{8,4},{9,13},{10,... | collective-permute-start | bytes 786440 | tf_op jit(solution)/shard_map/ppermute | solution.py:418
  36.2 0.7 copy-done.3
  36.9 0.8 copy-done.5
  37.6 1.5 %prepare.1 = (bf16[256,240]{1,0:T(8,128)(2,1)S(1)}, bf16[160,256]{1,0:T(8,128)(2,1)S(1)}, f32[1,4096]{1,0:T(1,128)S(1)}, f32[64,128]{1,0:T(8,128)S(1)}, f32[32,4096]{1,0:T(8,128)S(1)}) custom-call(s32[4,1,5]{2,1,0:T(1,128)S(1)} %copy-done.6, f32[4,5,4,64]{3,2,1,0:T(4,128)S(1)} %copy-done.5, s32[1,64]{1,0:T(1,128)S(1)} %copy-done.8, ...), custom_call_target="tpu_custom_call", output_to_operand_aliasing={{4}: (6, {})} | custom-call | flops 1000000 | bytes 1048576 | tf_op jit(solution)/shard_map/prepare/pallas_call | solution.py:210
  39.1 0.1 collective-permute-start.5
  39.2 0.1 collective-permute-done.6.refs_2_
  39.3 0.8 collective-permute-done.7.refs_3_
  40.2 4.7 %detector.1 = (f32[16,4096]{1,0:T(8,128)S(1)}, f32[16,4096]{1,0:T(8,128)S(1)}, f32[16,4096]{1,0:T(8,128)S(1)}, f32[16,4096]{1,0:T(8,128)S(1)}, f32[16,4096]{1,0:T(8,128)S(1)}, /*index=5*/f32[2,4096]{1,0:T(2,128)S(1)}) custom-call(bf16[256,240]{1,0:T(8,128)(2,1)S(1)} %get-tuple-element.29.ahead, bf16[160,256]{1,0:T(8,128)(2,1)S(1)} %get-tuple-element.30.back, ...), custom_call_target="tpu_custom_call" | custom-call | flops 251658240 | bytes 8388608 | tf_op jit(solution)/shard_map/detector/pallas_call | solution.py:260
  44.9 6.8 %collective-permute-start.8 = (f32[16,4096]{1,0:T(8,128)S(1)}, f32[16,4096]{1,0:T(8,128)S(1)}, u32[]{:S(2)}, u32[]{:S(2)}) collective-permute-start(f32[16,4096]{1,0:T(8,128)S(1)} %get-tuple-element.33), channel_id=1, source_target_pairs={{0,1},{1,5},{2,3},{3,7},{4,0},{5,9},{6,2},{7,11},{8,4},{9,13},{10,... | collective-permute-start | bytes 786440 | tf_op jit(solution)/shard_map/ppermute | solution.py:418
  51.7 0.0 collective-permute-start.11
  51.7 0.4 scatter.1
  52.1 2.5 %collective-permute-start.9 = (f32[64,128]{1,0:T(8,128)S(1)}, f32[64,128]{1,0:T(8,128)S(1)}, u32[]{:S(2)}, u32[]{:S(2)}) collective-permute-start(f32[64,128]{1,0:T(8,128)S(1)} %scatter.1), channel_id=1, source_target_pairs={{0,1},{1,0},{2,3},{3,2},{4,5},{5,4},{6,7},{7,6},{8,9},{9,8},{10,11... | collective-permute-start | bytes 98312 | tf_op jit(solution)/shard_map/ppermute | solution.py:418
  54.5 0.9 collective-permute-done.9
  55.4 1.2 %collective-permute-done.8.refs_1_ = f32[16,4096]{1,0:T(8,128)S(1)} collective-permute-done((f32[16,4096]{1,0:T(8,128)S(1)}, f32[16,4096]{1,0:T(8,128)S(1)}, u32[]{:S(2)}, u32[]{:S(2)}) %collective-permute-start.8) | collective-permute-done | bytes 262176 | tf_op jit(solution)/shard_map/ppermute | solution.py:418
  56.6 0.0 collective-permute-done.5.refs_3_.leading
  56.6 6.9 %collective-permute-start.10 = (f32[32,4096]{1,0:T(8,128)S(1)}, f32[32,4096]{1,0:T(8,128)S(1)}, u32[]{:S(2)}, u32[]{:S(2)}) collective-permute-start(f32[32,4096]{1,0:T(8,128)S(1)} %get-tuple-element.37), channel_id=1, source_target_pairs={{0,1},{1,5},{2,3},{3,7},{4,0},{5,9},{6,2},{7,11},{8,4},{9,13},{10,... | collective-permute-start | bytes 1572872 | tf_op jit(solution)/shard_map/ppermute | solution.py:418
  63.5 0.0 collective-permute-done.11.refs_1_
  63.5 0.1 collective-permute-start.12
  63.6 6.2 %collective-permute-start.13 = (f32[16,4096]{1,0:T(8,128)S(1)}, f32[16,4096]{1,0:T(8,128)S(1)}, u32[]{:S(2)}, u32[]{:S(2)}) collective-permute-start(f32[16,4096]{1,0:T(8,128)S(1)} %get-tuple-element.41.refs_3_), channel_id=1, source_target_pairs={{0,1},{1,5},{2,3},{3,7},{4,0},{5,9},{6,2},{7,11},{8,4},{9,13},{10,... | collective-permute-start | bytes 786440 | tf_op jit(solution)/shard_map/ppermute | solution.py:418
  69.9 2.6 %collective-permute-start.14 = (f32[64,128]{1,0:T(8,128)S(1)}, f32[64,128]{1,0:T(8,128)S(1)}, u32[]{:S(2)}, u32[]{:S(2)}) collective-permute-start(f32[64,128]{1,0:T(8,128)S(1)} %add.31.refs_2_.refs_0_), channel_id=1, source_target_pairs={{0,2},{1,3},{2,0},{3,1},{4,6},{5,7},{6,4},{7,5},{8,10},{9,11},{10,... | collective-permute-start | bytes 98312 | tf_op jit(solution)/shard_map/ppermute | solution.py:418
  72.4 2.9 %collective-permute-done.14.refs_1_ = f32[64,128]{1,0:T(8,128)S(1)} collective-permute-done((f32[64,128]{1,0:T(8,128)S(1)}, f32[64,128]{1,0:T(8,128)S(1)}, u32[]{:S(2)}, u32[]{:S(2)}) %collective-permute-start.14) | collective-permute-done | bytes 32800 | tf_op jit(solution)/shard_map/ppermute | solution.py:418
  75.3 3.9 %collective-permute-done.15 = f32[64,128]{1,0:T(8,128)S(1)} collective-permute-done((f32[64,128]{1,0:T(8,128)S(1)}, f32[64,128]{1,0:T(8,128)S(1)}, u32[]{:S(2)}, u32[]{:S(2)}) %collective-permute-start.15) | collective-permute-done | bytes 32800 | tf_op jit(solution)/shard_map/ppermute | solution.py:418
  79.3 2.7 %collective-permute-start.16 = (f32[16,4096]{1,0:T(8,128)S(1)}, f32[16,4096]{1,0:T(8,128)S(1)}, u32[]{:S(2)}, u32[]{:S(2)}) collective-permute-start(f32[16,4096]{1,0:T(8,128)S(1)} %add.48.rest_0_.refs_3_.refs_2_), channel_id=1, source_target_pairs={{0,2},{1,3},{2,0},{3,1},{4,6},{5,7},{6,4},{7,5},{8,10},{9,11},{10,... | collective-permute-start | bytes 786440 | tf_op jit(solution)/shard_map/ppermute | solution.py:418
  82.0 2.6 %smooth.1.base.refs_3_ = f32[4,32,4096]{2,1,0:T(8,128)S(1)} custom-call(f32[4,32,4096]{2,1,0:T(8,128)S(1)} %copy-done, f32[32,4096]{1,0:T(8,128)S(1)} %collective-permute-done.5.refs_3_.leading, f32[32,4096]{1,0:T(8,128)S(1)} %collective-permute-done.10.trailing, f32[16,4096]{1,0:T(8,128)S(1)} %add.48.rest_0_.refs_3_.refs_2_), custom_call_target="tpu_custom_call" | custom-call | flops 20971520 | bytes 5242880 | tf_op jit(solution)/shard_map/smooth/pallas_call | solution.py:350
  84.6 0.0 copy-start.4
  84.6 2.8 %collective-permute-done.19.refs_1_ = f32[64,128]{1,0:T(8,128)S(1)} collective-permute-done((f32[64,128]{1,0:T(8,128)S(1)}, f32[64,128]{1,0:T(8,128)S(1)}, u32[]{:S(2)}, u32[]{:S(2)}) %collective-permute-start.19) | collective-permute-done | bytes 32800 | tf_op jit(solution)/shard_map/ppermute | solution.py:418
  87.4 3.9 %collective-permute-done.20 = f32[64,128]{1,0:T(8,128)S(1)} collective-permute-done((f32[64,128]{1,0:T(8,128)S(1)}, f32[64,128]{1,0:T(8,128)S(1)}, u32[]{:S(2)}, u32[]{:S(2)}) %collective-permute-start.20) | collective-permute-done | bytes 32800 | tf_op jit(solution)/shard_map/ppermute | solution.py:418
  91.3 3.9 %collective-permute-done.21 = f32[64,128]{1,0:T(8,128)S(1)} collective-permute-done((f32[64,128]{1,0:T(8,128)S(1)}, f32[64,128]{1,0:T(8,128)S(1)}, u32[]{:S(2)}, u32[]{:S(2)}) %collective-permute-start.21) | collective-permute-done | bytes 32800 | tf_op jit(solution)/shard_map/ppermute | solution.py:418
  95.2 0.1 collective-permute-start.18
  95.3 0.5 collective-permute-start.17
  95.8 4.3 %collective-permute-done.22 = f32[64,128]{1,0:T(8,128)S(1)} collective-permute-done((f32[64,128]{1,0:T(8,128)S(1)}, f32[64,128]{1,0:T(8,128)S(1)}, u32[]{:S(2)}, u32[]{:S(2)}) %collective-permute-start.22) | collective-permute-done | bytes 32800 | tf_op jit(solution)/shard_map/ppermute | solution.py:418
  100.1 7.8 %collective-permute-done.23 = f32[64,128]{1,0:T(8,128)S(1)} collective-permute-done((f32[64,128]{1,0:T(8,128)S(1)}, f32[64,128]{1,0:T(8,128)S(1)}, u32[]{:S(2)}, u32[]{:S(2)}) %collective-permute-start.23) | collective-permute-done | bytes 32800 | tf_op jit(solution)/shard_map/ppermute | solution.py:418
  107.9 0.1 fusion
  108.0 0.1 reshape.7
  108.1 0.6 sub.3
  108.7 2.7 %update.1 = f32[4,32,4096]{2,1,0:T(8,128)} custom-call(f32[64,128]{1,0:T(8,128)S(1)} %get-tuple-element.22.weights, f32[4,32,4096]{2,1,0:T(8,128)S(1)} %smooth.1.base.refs_3_, f32[16,4096]{1,0:T(8,128)S(1)} %collective-permute-done.17.refs_0_, f32[16,4096]{1,0:T(8,128)S(1)} %collective-permute-done.18.refs_1_, ...), custom_call_target="tpu_custom_call" | custom-call | flops 201326592 | bytes 5242880 | tf_op jit(solution)/shard_map/update/pallas_call | solution.py:383
  (40 shorter events, 0.3 us)
Async XLA Ops:
  0.6 1.0 copy-start.2
  1.6 0.7 copy-start.7
  2.2 33.9 %copy-start.6 = (s32[4,1,5]{2,1,0:T(1,128)S(1)}, s32[4,1,5]{2,1,0:T(1,128)}, u32[]{:S(2)}) copy-start(s32[4,1,5]{2,1,0:T(1,128)} %incidence.1) | copy-start | bytes 244
  2.2 33.9 %copy-start.8 = (s32[1,64]{1,0:T(1,128)S(1)}, s32[1,64]{1,0:T(1,128)}, u32[]{:S(2)}) copy-start(s32[1,64]{1,0:T(1,128)} %gain_map.1) | copy-start | bytes 772
  2.2 37.9 %copy-start.1 = (f32[4,64,4096]{2,1,0:T(8,128)S(1)}, f32[4,64,4096]{2,1,0:T(8,128)}, u32[]{:S(2)}) copy-start(f32[4,64,4096]{2,1,0:T(8,128)} %measured.1) | copy-start | bytes 12582916
  4.7 1.6 %collective-permute-start.1 = (f32[16,4096]{1,0:T(8,128)S(1)}, f32[16,4096]{1,0:T(8,128)S(1)}, u32[]{:S(2)}, u32[]{:S(2)}) collective-permute-start(f32[16,4096]{1,0:T(8,128)S(1)} %get-tuple-element.26), channel_id=1, source_target_pairs={{0,1},{1,0},{2,3},{3,2},{4,5},{5,4},{6,7},{7,6},{8,9},{9,8},{10,11... | collective-permute-start | bytes 786440 | tf_op jit(solution)/shard_map/ppermute | solution.py:418
  4.8 3.9 %collective-permute-start = (f32[16,4096]{1,0:T(8,128)S(1)}, f32[16,4096]{1,0:T(8,128)S(1)}, u32[]{:S(2)}, u32[]{:S(2)}) collective-permute-start(f32[16,4096]{1,0:T(8,128)S(1)} %get-tuple-element.24), channel_id=1, source_target_pairs={{0,1},{1,0},{2,3},{3,2},{4,5},{5,4},{6,7},{7,6},{8,9},{9,8},{10,11... | collective-permute-start | bytes 786440 | tf_op jit(solution)/shard_map/ppermute | solution.py:418
  6.4 9.9 %collective-permute-start.2 = (f32[16,4096]{1,0:T(8,128)S(1)}, f32[16,4096]{1,0:T(8,128)S(1)}, u32[]{:S(2)}, u32[]{:S(2)}) collective-permute-start(f32[16,4096]{1,0:T(8,128)S(1)} %add.43), channel_id=1, source_target_pairs={{0,2},{1,3},{2,0},{3,1},{4,6},{5,7},{6,4},{7,5},{8,10},{9,11},{10,... | collective-permute-start | bytes 786440 | tf_op jit(solution)/shard_map/ppermute | solution.py:418
  16.4 12.4 %collective-permute-start.3 = (f32[16,4096]{1,0:T(8,128)S(1)}, f32[16,4096]{1,0:T(8,128)S(1)}, u32[]{:S(2)}, u32[]{:S(2)}) collective-permute-start(f32[16,4096]{1,0:T(8,128)S(1)} %add.44.refs_4_), channel_id=1, source_target_pairs={{0,4},{1,0},{2,6},{3,2},{4,8},{5,1},{6,10},{7,3},{8,12},{9,5},{10,... | collective-permute-start | bytes 786440 | tf_op jit(solution)/shard_map/ppermute | solution.py:418
  18.4 11.1 %collective-permute-start.4 = (f32[16,4096]{1,0:T(8,128)S(1)}, f32[16,4096]{1,0:T(8,128)S(1)}, u32[]{:S(2)}, u32[]{:S(2)}) collective-permute-start(f32[16,4096]{1,0:T(8,128)S(1)} %add.44.refs_4_), channel_id=1, source_target_pairs={{0,1},{1,5},{2,3},{3,7},{4,0},{5,9},{6,2},{7,11},{8,4},{9,13},{10,... | collective-permute-start | bytes 786440 | tf_op jit(solution)/shard_map/ppermute | solution.py:418
  28.8 10.6 %collective-permute-start.6 = (f32[16,4096]{1,0:T(8,128)S(1)}, f32[16,4096]{1,0:T(8,128)S(1)}, u32[]{:S(2)}, u32[]{:S(2)}) collective-permute-start(f32[16,4096]{1,0:T(8,128)S(1)} %collective-permute-done.3.rest_0_.refs_0_), channel_id=1, source_target_pairs={{0,4},{1,0},{2,6},{3,2},{4,8},{5,1},{6,10},{7,3},{8,12},{9,5},{10,... | collective-permute-start | bytes 786440 | tf_op jit(solution)/shard_map/ppermute | solution.py:418
  29.4 10.7 %collective-permute-start.7 = (f32[16,4096]{1,0:T(8,128)S(1)}, f32[16,4096]{1,0:T(8,128)S(1)}, u32[]{:S(2)}, u32[]{:S(2)}) collective-permute-start(f32[16,4096]{1,0:T(8,128)S(1)} %collective-permute-done.4.rest_1_.refs_1_), channel_id=1, source_target_pairs={{0,1},{1,5},{2,3},{3,7},{4,0},{5,9},{6,2},{7,11},{8,4},{9,13},{10,... | collective-permute-start | bytes 786440 | tf_op jit(solution)/shard_map/ppermute | solution.py:418
  36.2 0.7 copy-start.3
  36.9 0.8 copy-start.5
  39.1 17.5 %collective-permute-start.5 = (f32[32,4096]{1,0:T(8,128)S(1)}, f32[32,4096]{1,0:T(8,128)S(1)}, u32[]{:S(2)}, u32[]{:S(2)}) collective-permute-start(f32[32,4096]{1,0:T(8,128)S(1)} %get-tuple-element.28), channel_id=1, source_target_pairs={{0,4},{1,0},{2,6},{3,2},{4,8},{5,1},{6,10},{7,3},{8,12},{9,5},{10,... | collective-permute-start | bytes 1572872 | tf_op jit(solution)/shard_map/ppermute | solution.py:418
  44.9 11.7 %collective-permute-start.8 = (f32[16,4096]{1,0:T(8,128)S(1)}, f32[16,4096]{1,0:T(8,128)S(1)}, u32[]{:S(2)}, u32[]{:S(2)}) collective-permute-start(f32[16,4096]{1,0:T(8,128)S(1)} %get-tuple-element.33), channel_id=1, source_target_pairs={{0,1},{1,5},{2,3},{3,7},{4,0},{5,9},{6,2},{7,11},{8,4},{9,13},{10,... | collective-permute-start | bytes 786440 | tf_op jit(solution)/shard_map/ppermute | solution.py:418
  51.7 11.8 %collective-permute-start.11 = (f32[16,4096]{1,0:T(8,128)S(1)}, f32[16,4096]{1,0:T(8,128)S(1)}, u32[]{:S(2)}, u32[]{:S(2)}) collective-permute-start(f32[16,4096]{1,0:T(8,128)S(1)} %get-tuple-element.40), channel_id=1, source_target_pairs={{0,4},{1,0},{2,6},{3,2},{4,8},{5,1},{6,10},{7,3},{8,12},{9,5},{10,... | collective-permute-start | bytes 786440 | tf_op jit(solution)/shard_map/ppermute | solution.py:418
  52.1 3.3 %collective-permute-start.9 = (f32[64,128]{1,0:T(8,128)S(1)}, f32[64,128]{1,0:T(8,128)S(1)}, u32[]{:S(2)}, u32[]{:S(2)}) collective-permute-start(f32[64,128]{1,0:T(8,128)S(1)} %scatter.1), channel_id=1, source_target_pairs={{0,1},{1,0},{2,3},{3,2},{4,5},{5,4},{6,7},{7,6},{8,9},{9,8},{10,11... | collective-permute-start | bytes 98312 | tf_op jit(solution)/shard_map/ppermute | solution.py:418
  56.6 25.3 %copy-start = (f32[4,32,4096]{2,1,0:T(8,128)S(1)}, f32[4,32,4096]{2,1,0:T(8,128)}, u32[]{:S(2)}) copy-start(f32[4,32,4096]{2,1,0:T(8,128)} %volume.3) | copy-start | bytes 6291460
  56.6 25.3 %collective-permute-start.10 = (f32[32,4096]{1,0:T(8,128)S(1)}, f32[32,4096]{1,0:T(8,128)S(1)}, u32[]{:S(2)}, u32[]{:S(2)}) collective-permute-start(f32[32,4096]{1,0:T(8,128)S(1)} %get-tuple-element.37), channel_id=1, source_target_pairs={{0,1},{1,5},{2,3},{3,7},{4,0},{5,9},{6,2},{7,11},{8,4},{9,13},{10,... | collective-permute-start | bytes 1572872 | tf_op jit(solution)/shard_map/ppermute | solution.py:418
  63.5 15.7 %collective-permute-start.12 = (f32[16,4096]{1,0:T(8,128)S(1)}, f32[16,4096]{1,0:T(8,128)S(1)}, u32[]{:S(2)}, u32[]{:S(2)}) collective-permute-start(f32[16,4096]{1,0:T(8,128)S(1)} %add.46.refs_2_), channel_id=1, source_target_pairs={{0,4},{1,0},{2,6},{3,2},{4,8},{5,1},{6,10},{7,3},{8,12},{9,5},{10,... | collective-permute-start | bytes 786440 | tf_op jit(solution)/shard_map/ppermute | solution.py:418
  63.6 15.6 %collective-permute-start.13 = (f32[16,4096]{1,0:T(8,128)S(1)}, f32[16,4096]{1,0:T(8,128)S(1)}, u32[]{:S(2)}, u32[]{:S(2)}) collective-permute-start(f32[16,4096]{1,0:T(8,128)S(1)} %get-tuple-element.41.refs_3_), channel_id=1, source_target_pairs={{0,1},{1,5},{2,3},{3,7},{4,0},{5,9},{6,2},{7,11},{8,4},{9,13},{10,... | collective-permute-start | bytes 786440 | tf_op jit(solution)/shard_map/ppermute | solution.py:418
  69.9 5.4 %collective-permute-start.14 = (f32[64,128]{1,0:T(8,128)S(1)}, f32[64,128]{1,0:T(8,128)S(1)}, u32[]{:S(2)}, u32[]{:S(2)}) collective-permute-start(f32[64,128]{1,0:T(8,128)S(1)} %add.31.refs_2_.refs_0_), channel_id=1, source_target_pairs={{0,2},{1,3},{2,0},{3,1},{4,6},{5,7},{6,4},{7,5},{8,10},{9,11},{10,... | collective-permute-start | bytes 98312 | tf_op jit(solution)/shard_map/ppermute | solution.py:418
  75.3 3.9 %collective-permute-start.15 = (f32[64,128]{1,0:T(8,128)S(1)}, f32[64,128]{1,0:T(8,128)S(1)}, u32[]{:S(2)}, u32[]{:S(2)}) collective-permute-start(f32[64,128]{1,0:T(8,128)S(1)} %add.47), channel_id=1, source_target_pairs={{0,32},{1,33},{2,34},{3,35},{4,36},{5,37},{6,38},{7,39},{8,40},{9,... | collective-permute-start | bytes 98312 | tf_op jit(solution)/shard_map/ppermute | solution.py:418
  79.3 16.0 %collective-permute-start.16 = (f32[16,4096]{1,0:T(8,128)S(1)}, f32[16,4096]{1,0:T(8,128)S(1)}, u32[]{:S(2)}, u32[]{:S(2)}) collective-permute-start(f32[16,4096]{1,0:T(8,128)S(1)} %add.48.rest_0_.refs_3_.refs_2_), channel_id=1, source_target_pairs={{0,2},{1,3},{2,0},{3,1},{4,6},{5,7},{6,4},{7,5},{8,10},{9,11},{10,... | collective-permute-start | bytes 786440 | tf_op jit(solution)/shard_map/ppermute | solution.py:418
  81.9 5.4 %collective-permute-start.19 = (f32[64,128]{1,0:T(8,128)S(1)}, f32[64,128]{1,0:T(8,128)S(1)}, u32[]{:S(2)}, u32[]{:S(2)}) collective-permute-start(f32[64,128]{1,0:T(8,128)S(1)} %add.32.refs_3_.refs_0_), channel_id=1, source_target_pairs={{0,64},{1,65},{2,66},{3,67},{4,68},{5,69},{6,70},{7,71},{8,72},{9,... | collective-permute-start | bytes 98312 | tf_op jit(solution)/shard_map/ppermute | solution.py:418
  84.6 23.5 %copy-start.4 = (f32[4096]{0:T(1024)S(1)}, f32[4096]{0:T(1024)}, u32[]{:S(2)}) copy-start(f32[4096]{0:T(1024)} %gain_values.1) | copy-start | bytes 49156
  87.4 3.9 %collective-permute-start.20 = (f32[64,128]{1,0:T(8,128)S(1)}, f32[64,128]{1,0:T(8,128)S(1)}, u32[]{:S(2)}, u32[]{:S(2)}) collective-permute-start(f32[64,128]{1,0:T(8,128)S(1)} %add.49), channel_id=1, source_target_pairs={{0,128},{1,129},{2,130},{3,131},{4,132},{5,133},{6,134},{7,135},{8... | collective-permute-start | bytes 98312 | tf_op jit(solution)/shard_map/ppermute | solution.py:418
  91.3 3.9 %collective-permute-start.21 = (f32[64,128]{1,0:T(8,128)S(1)}, f32[64,128]{1,0:T(8,128)S(1)}, u32[]{:S(2)}, u32[]{:S(2)}) collective-permute-start(f32[64,128]{1,0:T(8,128)S(1)} %add.33), channel_id=1, source_target_pairs={{0,4},{1,5},{2,6},{3,7},{4,0},{5,1},{6,2},{7,3},{8,12},{9,13},{10,... | collective-permute-start | bytes 98312 | tf_op jit(solution)/shard_map/ppermute | solution.py:418
  95.2 4.9 %collective-permute-start.22 = (f32[64,128]{1,0:T(8,128)S(1)}, f32[64,128]{1,0:T(8,128)S(1)}, u32[]{:S(2)}, u32[]{:S(2)}) collective-permute-start(f32[64,128]{1,0:T(8,128)S(1)} %add.34), channel_id=1, source_target_pairs={{0,8},{1,9},{2,10},{3,11},{4,12},{5,13},{6,14},{7,15},{8,0},{9,1},... | collective-permute-start | bytes 98312 | tf_op jit(solution)/shard_map/ppermute | solution.py:418
  95.2 13.5 %collective-permute-start.18 = (f32[16,4096]{1,0:T(8,128)S(1)}, f32[16,4096]{1,0:T(8,128)S(1)}, u32[]{:S(2)}, u32[]{:S(2)}) collective-permute-start(f32[16,4096]{1,0:T(8,128)S(1)} %add.48.rest_0_.refs_3_.refs_2_), channel_id=1, source_target_pairs={{0,1},{1,0},{2,3},{3,2},{4,5},{5,4},{6,7},{7,6},{8,9},{9,8},{10,11... | collective-permute-start | bytes 786440 | tf_op jit(solution)/shard_map/ppermute | solution.py:418
  95.3 13.4 %collective-permute-start.17 = (f32[16,4096]{1,0:T(8,128)S(1)}, f32[16,4096]{1,0:T(8,128)S(1)}, u32[]{:S(2)}, u32[]{:S(2)}) collective-permute-start(f32[16,4096]{1,0:T(8,128)S(1)} %collective-permute-done.16.refs_2_), channel_id=1, source_target_pairs={{0,1},{1,0},{2,3},{3,2},{4,5},{5,4},{6,7},{7,6},{8,9},{9,8},{10,11... | collective-permute-start | bytes 786440 | tf_op jit(solution)/shard_map/ppermute | solution.py:418
  100.1 7.8 %collective-permute-start.23 = (f32[64,128]{1,0:T(8,128)S(1)}, f32[64,128]{1,0:T(8,128)S(1)}, u32[]{:S(2)}, u32[]{:S(2)}) collective-permute-start(f32[64,128]{1,0:T(8,128)S(1)} %add.35), channel_id=1, source_target_pairs={{0,16},{1,17},{2,18},{3,19},{4,20},{5,21},{6,22},{7,23},{8,24},{9,... | collective-permute-start | bytes 98312 | tf_op jit(solution)/shard_map/ppermute | solution.py:418
